TPU v7x, 32 devices: a whole 2x2x4 slice. The times are simulated.
32 devices in a mesh: seq: 8 (over z, x), head: 4 (over y, core).
Axes of the slice: x: 2, y: 2, z: 4, core: 2. Of those that a mesh axis runs over, the one named last changes fastest.
Arguments:
- queries: bfloat16 [8192, 4096], P(('seq', 'head')), may hold values from -10 to 10
- key_rows: bfloat16 [8192, 4096], P(('seq', 'head')), may hold values from -10 to 10
- value_rows: bfloat16 [8192, 4096], P(('seq', 'head')), may hold values from -6 to 6
- cotangent: bfloat16 [8192, 4096], P(('seq', 'head')), may hold values from -6 to 6
- neighbours: int32 [64, 8], replicated, may hold values from 0 to 63, as said below
- counts: int32 [64], replicated, may hold values from 2 to 8, as said below
Outputs:
- attended: bfloat16 [8192, 4096], P(('seq', 'head'))
- grad_queries: bfloat16 [8192, 4096], P(('seq', 'head'))
- grad_keys: bfloat16 [8192, 4096], P(('seq', 'head'))
- grad_values: bfloat16 [8192, 4096], P(('seq', 'head'))
Inputs may be any that keep to these rules, and one draw needn't show every extreme that they name: `neighbours`: row b holds 8 different block numbers: the first is b, the second is b + 8 modulo 64 for even b and b - 8 modulo 64 for odd b, every other is b + o modulo 64 with 1 <= |o| <= 8. Only the first counts[b] slots of row b are used; some block uses all and some uses 2.
All inputs are finite; a program needn't handle non-finite values.
Results may differ from a plain program's by a relative error of at most 0.025.
Values may be sent and summed in bfloat16 or wider, within the bound.
A program may use at most 192 MiB of HBM per device.

v0:
```python
import jax
import jax.numpy as jnp
from jax import lax
from jax.sharding import PartitionSpec as P

HEAD_DIM = 128
BLOCK = 128


def with_halo(block, sides, width):
    for axis, dim in sides:
        count = lax.axis_size(axis)
        forward = [(i, i + 1) for i in range(count - 1)]
        forward.append((count - 1, 0))
        backward = [(target, source) for source, target in forward]
        low = lax.ppermute(
            lax.slice_in_dim(block, block.shape[dim] - width, None, axis=dim), axis, forward
        )
        high = lax.ppermute(lax.slice_in_dim(block, 0, width, axis=dim), axis, backward)
        block = jnp.concatenate([low, block, high], axis=dim)
    return block


def passed_along(value, axis, steps):
    count = lax.axis_size(axis)
    pairs = [(source, (source + steps) % count) for source in range(count)]
    return lax.ppermute(value, axis, pairs)


def score_tile(q_tile, key_tiles, valid):
    scale = HEAD_DIM ** (-0.5)
    scores = (
        jnp.einsum("qhd,nkhd->hqnk", q_tile, key_tiles, preferred_element_type=jnp.float32) * scale
    )
    return jnp.where(valid[None, None, :, None], scores, -jnp.inf)


def tile_grads(weights, q_tile, g_tile, value_tiles, inner):
    scale = HEAD_DIM ** (-0.5)
    weights_low = weights.astype(jnp.bfloat16)
    grad_weights = jnp.einsum(
        "qhd,nkhd->hqnk", g_tile, value_tiles, preferred_element_type=jnp.float32
    )
    grad_scores = weights * (grad_weights - inner[:, :, None, None])
    grad_low = grad_scores.astype(jnp.bfloat16)
    key_part = scale * jnp.einsum(
        "hqnk,qhd->nkhd", grad_low, q_tile, preferred_element_type=jnp.float32
    )
    value_part = jnp.einsum(
        "hqnk,qhd->nkhd", weights_low, g_tile, preferred_element_type=jnp.float32
    )
    return (grad_low, key_part, value_part)


def attend_tile(q_tile, g_tile, key_tiles, value_tiles, valid):
    scale = HEAD_DIM ** (-0.5)
    scores = score_tile(q_tile, key_tiles, valid)
    highest = jnp.max(scores, axis=(2, 3), keepdims=True)
    raised = jnp.exp(scores - highest)
    totals = jnp.sum(raised, axis=(2, 3), keepdims=True)
    weights = raised / totals
    weights_low = weights.astype(jnp.bfloat16)
    attended = jnp.einsum(
        "hqnk,nkhd->qhd", weights_low, value_tiles, preferred_element_type=jnp.float32
    ).astype(jnp.bfloat16)
    inner = jnp.sum(g_tile.astype(jnp.float32) * attended.astype(jnp.float32), axis=2).T
    grad_low, key_part, value_part = tile_grads(weights, q_tile, g_tile, value_tiles, inner)
    grad_query = (
        scale
        * jnp.einsum("hqnk,nkhd->qhd", grad_low, key_tiles, preferred_element_type=jnp.float32)
    ).astype(jnp.bfloat16)
    log_total = highest[:, :, 0, 0] + jnp.log(totals[:, :, 0, 0])
    return (attended, grad_query, key_part, value_part, log_total, inner)


def local(queries, key_rows, value_rows, cotangent, neighbours, counts):
    q_seq, k_seq, v_seq, g_seq = (
        lax.all_to_all(queries, "head", split_axis=1, concat_axis=0, tiled=True),
        lax.all_to_all(key_rows, "head", split_axis=1, concat_axis=0, tiled=True),
        lax.all_to_all(value_rows, "head", split_axis=1, concat_axis=0, tiled=True),
        lax.all_to_all(cotangent, "head", split_axis=1, concat_axis=0, tiled=True),
    )
    tok_seq = q_seq.shape[0]
    width = q_seq.shape[1]
    heads_here = width // HEAD_DIM
    blocks_here = tok_seq // BLOCK
    total_blocks = neighbours.shape[0]
    slot_count = neighbours.shape[1]
    first_block = lax.axis_index("seq") * blocks_here
    tile_shape = (blocks_here, BLOCK, heads_here, HEAD_DIM)
    own_lists = lax.dynamic_slice_in_dim(neighbours, first_block, blocks_here, 0)
    own_counts = lax.dynamic_slice_in_dim(counts, first_block, blocks_here, 0)
    slot_index = jnp.arange(slot_count, dtype=jnp.int32)
    key_value = jnp.stack((k_seq, v_seq), 0)
    window = with_halo(key_value, (("seq", 1),), tok_seq)
    window = window.reshape((2, 3 * blocks_here, BLOCK, heads_here, HEAD_DIM))
    key_window = window[0]
    value_window = window[1]
    window_ids = (own_lists - first_block + blocks_here) % total_blocks
    zero_window = jnp.zeros((3 * blocks_here, BLOCK, heads_here, HEAD_DIM), jnp.float32)

    def visit(running, inputs):
        grad_k, grad_v = running
        q_tile, g_tile, tile_ids, tile_count = inputs
        outcome = attend_tile(
            q_tile, g_tile, key_window[tile_ids], value_window[tile_ids], slot_index < tile_count
        )
        grad_k = grad_k.at[tile_ids].add(outcome[2])
        grad_v = grad_v.at[tile_ids].add(outcome[3])
        return ((grad_k, grad_v), (outcome[0], outcome[1], outcome[4], outcome[5]))

    (grad_k, grad_v), (attended, grad_query, log_totals, inners) = lax.scan(
        visit,
        (zero_window, zero_window),
        (q_seq.reshape(tile_shape), g_seq.reshape(tile_shape), window_ids, own_counts),
    )
    middle_k = grad_k[blocks_here : 2 * blocks_here]
    middle_v = grad_v[blocks_here : 2 * blocks_here]
    lower_part = jnp.stack((grad_k[:blocks_here], grad_v[:blocks_here]), 0)
    upper_part = jnp.stack((grad_k[2 * blocks_here :], grad_v[2 * blocks_here :]), 0)
    from_next = passed_along(lower_part, "seq", -1)
    from_prev = passed_along(upper_part, "seq", 1)
    own_k = middle_k + from_next[0] + from_prev[0]
    own_v = middle_v + from_next[1] + from_prev[1]
    grad_k_rows = own_k.reshape((tok_seq, width)).astype(jnp.bfloat16)
    grad_v_rows = own_v.reshape((tok_seq, width)).astype(jnp.bfloat16)
    return (
        lax.all_to_all(
            attended.reshape((tok_seq, width)), "head", split_axis=0, concat_axis=1, tiled=True
        ),
        lax.all_to_all(
            grad_query.reshape((tok_seq, width)), "head", split_axis=0, concat_axis=1, tiled=True
        ),
        lax.all_to_all(grad_k_rows, "head", split_axis=0, concat_axis=1, tiled=True),
        lax.all_to_all(grad_v_rows, "head", split_axis=0, concat_axis=1, tiled=True),
    )


def solution(mesh):
    in_specs = (
        P(("seq", "head"), None),
        P(("seq", "head"), None),
        P(("seq", "head"), None),
        P(("seq", "head"), None),
        P(),
        P(),
    )
    out_specs = (
        P(("seq", "head"), None),
        P(("seq", "head"), None),
        P(("seq", "head"), None),
        P(("seq", "head"), None),
    )
    return jax.shard_map(local, mesh=mesh, in_specs=in_specs, out_specs=out_specs, check_vma=False)
```

profile of v0, /device:TPU:23, one launch (start us, length us, event | category | flops | bytes accessed | tf_op | source)
XLA Modules:
  0.0 1186.4 jit_solution(11655471245949793243)
XLA Ops:
  18.7 15.8 %all-to-all-done.1 = bf16[256,4,1024]{2,0,1:T(8,128)(2,1)S(1)} async-done(((bf16[256,4,1024]{2,0,1:T(8,128)(2,1)}), bf16[256,4,1024]{2,0,1:T(8,128)(2,1)S(1)}, u32[]{:S(2)}, u32[]{:S(2)}) %all-to-all-start.1) | async-done | bytes 2097184 | tf_op jit(solution)/shard_map/all_to_all | solution.py:79
  34.5 29.3 %all_to_all.134 = bf16[256,4,1024]{2,0,1:T(8,128)(2,1)S(1)} all-to-all(bf16[256,4,1024]{2,0,1:T(8,128)(2,1)} %copy.136), channel_id=1, replica_groups=mesh['seq'=8,'head'=4] {'head'}, dimensions={1} | all-to-all | bytes 4194304 | tf_op jit(solution)/shard_map/all_to_all | solution.py:80
  80.5 20.7 %all-to-all-done = bf16[256,4,1024]{2,0,1:T(8,128)(2,1)} async-done(((bf16[256,4,1024]{2,0,1:T(8,128)(2,1)}), bf16[256,4,1024]{2,0,1:T(8,128)(2,1)}, u32[]{:S(2)}, u32[]{:S(2)}) %all-to-all-start) | async-done | bytes 2097184 | tf_op jit(solution)/shard_map/all_to_all | solution.py:78
  111.4 20.1 %all-to-all-done.3 = bf16[256,4,1024]{2,0,1:T(8,128)(2,1)} async-done(((bf16[256,4,1024]{2,0,1:T(8,128)(2,1)}), bf16[256,4,1024]{2,0,1:T(8,128)(2,1)}, u32[]{:S(2)}, u32[]{:S(2)}) %all-to-all-start.3) | async-done | bytes 2097184 | tf_op jit(solution)/shard_map/all_to_all | solution.py:81
  135.2 111.1 %collective-permute-done.1 = bf16[2,1024,1024]{2,1,0:T(8,128)(2,1)} collective-permute-done((bf16[2,1024,1024]{2,1,0:T(8,128)(2,1)}, bf16[2,1024,1024]{2,1,0:T(8,128)(2,1)}, u32[]{:S(2)}, u32[]{:S(2)}) %collective-permute-start.1) | collective-permute-done | bytes 4194336 | tf_op jit(solution)/shard_map/ppermute | solution.py:19
  279.9 453.6 %while.17 = (s32[]{:T(128)}, f32[24,128,8,128]{3,2,1,0:T(8,128)}, f32[24,128,8,128]{3,2,1,0:T(8,128)}, bf16[8,128,8,128]{3,2,1,0:T(8,128)(2,1)}, bf16[8,128,8,12...) while((s32[]{:T(128)}, f32[24,128,8,128]{3,2,1,0:T(8,128)}, ...), condition=%wide.region_6.7_spmd.clone, body=%wide.region_0.6_spmd.clone.sunk | while | flops 1639839744 | bytes 132432376 | solution.py:112
  317.7 9.4 scatter_fusion
  327.1 9.5 scatter_fusion.1
  383.8 9.5 scatter_fusion.1
  431.0 9.5 scatter_fusion
  440.5 9.4 scatter_fusion.1
  487.7 9.4 scatter_fusion
  544.3 9.5 scatter_fusion
  553.7 9.5 scatter_fusion.1
  601.0 9.6 scatter_fusion
  610.6 9.5 scatter_fusion.1
  657.8 9.5 scatter_fusion
  667.3 9.5 scatter_fusion.1
  714.6 9.5 scatter_fusion
  724.0 9.4 scatter_fusion.1
  761.9 19.7 %all-to-all-done.5 = bf16[4,256,1024]{2,1,0:T(8,128)(2,1)S(1)} async-done(((bf16[4,256,1024]{2,1,0:T(8,128)(2,1)}), bf16[4,256,1024]{2,1,0:T(8,128)(2,1)S(1)}, u32[]{:S(2)}, u32[]{:S(2)}) %all-to-all-start.5) | async-done | bytes 2097184 | tf_op jit(solution)/shard_map/all_to_all | solution.py:131
  787.8 317.0 %collective-permute-done.3 = f32[2,8,128,8,128]{4,3,2,1,0:T(8,128)} collective-permute-done((f32[2,8,128,8,128]{4,3,2,1,0:T(8,128)}, f32[2,8,128,8,128]{4,3,2,1,0:T(8,128)}, u32[]{:S(2)}, u32[]{:S(2)}) %collective-permute-start.3) | collective-permute-done | bytes 8388640 | tf_op jit(solution)/shard_map/ppermute | solution.py:27
  1104.8 10.2 fusion.25
  1128.8 21.6 %all-to-all-done.7 = bf16[4,256,1024]{2,1,0:T(8,128)(2,1)} async-done(((bf16[4,256,1024]{2,1,0:T(8,128)(2,1)}), bf16[4,256,1024]{2,1,0:T(8,128)(2,1)}, u32[]{:S(2)}, u32[]{:S(2)}) %all-to-all-start.7) | async-done | bytes 2097184 | tf_op jit(solution)/shard_map/all_to_all | solution.py:135
  (287 shorter events, 486.6 us)
Async XLA Ops:
  0.6 107.1 %copy-start = (s32[64,8]{0,1:T(8,128)S(1)}, s32[64,8]{0,1:T(8,128)}, u32[]{:S(2)}) copy-start(s32[64,8]{0,1:T(8,128)} %param.12) | copy-start | bytes 6148
  6.3 28.2 %all-to-all-start.1 = ((bf16[256,4,1024]{2,0,1:T(8,128)(2,1)}), bf16[256,4,1024]{2,0,1:T(8,128)(2,1)S(1)}, u32[]{:S(2)}, u32[]{:S(2)}) async-start(bf16[256,4,1024]{2,0,1:T(8,128)(2,1)} %copy.134), calls=%async_computation.1 | async-start | bytes 4194304 | tf_op jit(solution)/shard_map/all_to_all | solution.py:79
  66.6 179.8 %collective-permute-start.1 = (bf16[2,1024,1024]{2,1,0:T(8,128)(2,1)}, bf16[2,1024,1024]{2,1,0:T(8,128)(2,1)}, u32[]{:S(2)}, u32[]{:S(2)}) collective-permute-start(bf16[2,1024,1024]{2,1,0:T(8,128)(2,1)} %pad_maximum_fusion.3), channel_id=1, source_target_pairs={{4,0},{8,4},{12,8},{16,12},{20,16},{24,20},{28,24},{0,28},{5,1},{9... | collective-permute-start | bytes 12582920 | tf_op jit(solution)/shard_map/ppermute | solution.py:19
  66.9 182.0 %collective-permute-start = (bf16[2,1024,1024]{2,1,0:T(8,128)(2,1)}, bf16[2,1024,1024]{2,1,0:T(8,128)(2,1)}, u32[]{:S(2)}, u32[]{:S(2)}) collective-permute-start(bf16[2,1024,1024]{2,1,0:T(8,128)(2,1)} %pad_maximum_fusion.3), channel_id=1, source_target_pairs={{0,4},{4,8},{8,12},{12,16},{16,20},{20,24},{24,28},{28,0},{1,5},{5... | collective-permute-start | bytes 12582920 | tf_op jit(solution)/shard_map/ppermute | solution.py:16
  70.5 30.8 %all-to-all-start = ((bf16[256,4,1024]{2,0,1:T(8,128)(2,1)}), bf16[256,4,1024]{2,0,1:T(8,128)(2,1)}, u32[]{:S(2)}, u32[]{:S(2)}) async-start(bf16[256,4,1024]{2,0,1:T(8,128)(2,1)} %bitcast.229), calls=%async_computation | async-start | bytes 4194304 | tf_op jit(solution)/shard_map/all_to_all | solution.py:78
  77.4 30.3 %copy-start.11 = (s32[64]{0:T(128)S(1)}, s32[64]{0:T(128)}, u32[]{:S(2)}) copy-start(s32[64]{0:T(128)} %param.13) | copy-start | bytes 772
  101.3 30.3 %all-to-all-start.3 = ((bf16[256,4,1024]{2,0,1:T(8,128)(2,1)}), bf16[256,4,1024]{2,0,1:T(8,128)(2,1)}, u32[]{:S(2)}, u32[]{:S(2)}) async-start(bf16[256,4,1024]{2,0,1:T(8,128)(2,1)} %bitcast.228), calls=%async_computation.3 | async-start | bytes 4194304 | tf_op jit(solution)/shard_map/all_to_all | solution.py:81
  131.5 117.3 %copy-start.6 = (bf16[256,4,1024]{2,0,1:T(8,128)(2,1)S(1)}, bf16[256,4,1024]{2,0,1:T(8,128)(2,1)}, u32[]{:S(2)}) copy-start(bf16[256,4,1024]{2,0,1:T(8,128)(2,1)} %copy-done.5) | copy-start | bytes 6291460
  305.9 5.8 copy-start.3
  362.6 5.8 copy-start.3
  419.2 5.8 copy-start.3
  475.9 5.8 copy-start.3
  532.5 5.8 copy-start.3
  589.2 5.8 copy-start.3
  646.0 5.8 copy-start.3
  744.0 360.8 %collective-permute-start.3 = (f32[2,8,128,8,128]{4,3,2,1,0:T(8,128)}, f32[2,8,128,8,128]{4,3,2,1,0:T(8,128)}, u32[]{:S(2)}, u32[]{:S(2)}) collective-permute-start(f32[2,8,128,8,128]{4,3,2,1,0:T(8,128)} %pad_maximum_fusion.2), channel_id=1, source_target_pairs={{0,4},{4,8},{8,12},{12,16},{16,20},{20,24},{24,28},{28,0},{1,5},{5... | collective-permute-start | bytes 25165832 | tf_op jit(solution)/shard_map/ppermute | solution.py:27
  747.9 356.9 %collective-permute-start.2 = (f32[2,8,128,8,128]{4,3,2,1,0:T(8,128)}, f32[2,8,128,8,128]{4,3,2,1,0:T(8,128)}, u32[]{:S(2)}, u32[]{:S(2)}) collective-permute-start(f32[2,8,128,8,128]{4,3,2,1,0:T(8,128)} %pad_maximum_fusion.1), channel_id=1, source_target_pairs={{0,28},{4,0},{8,4},{12,8},{16,12},{20,16},{24,20},{28,24},{1,29},{... | collective-permute-start | bytes 25165832 | tf_op jit(solution)/shard_map/ppermute | solution.py:27
  751.5 30.1 %all-to-all-start.5 = ((bf16[4,256,1024]{2,1,0:T(8,128)(2,1)}), bf16[4,256,1024]{2,1,0:T(8,128)(2,1)S(1)}, u32[]{:S(2)}, u32[]{:S(2)}) async-start(bf16[4,256,1024]{2,1,0:T(8,128)(2,1)} %all_to_all.116), calls=%async_computation.5 | async-start | bytes 4194304 | tf_op jit(solution)/shard_map/all_to_all | solution.py:131
  781.6 323.2 %copy-start.7 = (bf16[4,256,1024]{2,1,0:T(8,128)(2,1)}, bf16[4,256,1024]{2,1,0:T(8,128)(2,1)S(1)}, u32[]{:S(2)}) copy-start(bf16[4,256,1024]{2,1,0:T(8,128)(2,1)S(1)} %all-to-all-done.5) | copy-start | bytes 6291460
  781.6 337.5 %all-to-all-start.4 = ((bf16[4,256,1024]{2,1,0:T(8,128)(2,1)}), bf16[4,256,1024]{2,1,0:T(8,128)(2,1)}, u32[]{:S(2)}, u32[]{:S(2)}) async-start(bf16[4,256,1024]{2,1,0:T(8,128)(2,1)} %all_to_all.112), calls=%async_computation.4 | async-start | bytes 4194304 | tf_op jit(solution)/shard_map/all_to_all | solution.py:128
  1119.2 31.3 %all-to-all-start.7 = ((bf16[4,256,1024]{2,1,0:T(8,128)(2,1)}), bf16[4,256,1024]{2,1,0:T(8,128)(2,1)}, u32[]{:S(2)}, u32[]{:S(2)}) async-start(bf16[4,256,1024]{2,1,0:T(8,128)(2,1)} %convert_element_type.42), calls=%async_computation.7 | async-start | bytes 4194304 | tf_op jit(solution)/shard_map/all_to_all | solution.py:135
  1128.8 28.0 %copy-start.8 = (bf16[4,256,1024]{2,1,0:T(8,128)(2,1)S(1)}, bf16[4,256,1024]{2,1,0:T(8,128)(2,1)}, u32[]{:S(2)}) copy-start(bf16[4,256,1024]{2,1,0:T(8,128)(2,1)} %copy-done.7) | copy-start | bytes 6291460
  1150.4 30.2 %all-to-all-start.6 = ((bf16[4,256,1024]{2,1,0:T(8,128)(2,1)}), bf16[4,256,1024]{2,1,0:T(8,128)(2,1)}, u32[]{:S(2)}, u32[]{:S(2)}) async-start(bf16[4,256,1024]{2,1,0:T(8,128)(2,1)} %convert_element_type.40), calls=%async_computation.6 | async-start | bytes 4194304 | tf_op jit(solution)/shard_map/all_to_all | solution.py:134
  1171.9 14.4 %copy-start.1 = (s32[64,8]{0,1:T(8,128)S(1)}, s32[64,8]{0,1:T(8,128)}, u32[]{:S(2)}) copy-start(s32[64,8]{0,1:T(8,128)} %param.12) | copy-start | bytes 6148
  (20 other events, 42.6 us)
where the time goes:
time: 1200 us; the launch traced here: 1190 us
  waiting for transfers between devices  534 us (44%)
  local copies, waits for them, and re-layouts  312 us (26%)
  other arithmetic  191 us (16%)
  matrix products  70.2 us (6%)
  starting transfers between devices  47.6 us (4%)
  blocking collectives  29.3 us (2%)
    ppermute x2, waiting for transfers between devices, passed_along(): return lax.ppermute(value, axis, pairs)  317 us
    ppermute x1, waiting for transfers between devices, with_halo(): lax.ppermute(lax.slice_in_dim(block, 0, width, axis=dim), axis, backward)  111 us
    scatter-add x8, other arithmetic, visit(): grad_k = grad_k.at[tile_ids].add(outcome[2])  75.8 us
    scatter-add x8, other arithmetic, visit(): grad_v = grad_v.at[tile_ids].add(outcome[3])  75.5 us
    gather x16, local copies, waits for them, and re-layouts, visit(): value_window[tile_ids]  72.7 us
    transpose x8, local copies, waits for them, and re-layouts, tile_grads(): jnp.einsum('hqnk,qhd->nkhd', weights_low, g_tile, preferred_element_type=...  44.5 us
    unnamed x30, local copies, waits for them, and re-layouts  39.5 us
    mul x8, local copies, waits for them, and re-layouts, tile_grads(): scale * jnp.einsum('hqnk,qhd->nkhd', grad_low, q_tile, preferred_element_...  34.5 us
  transfers between devices with their start and end apart: 11, of which 9 were waited for; matrix products, arithmetic and copies ran while one was open for 5% of the time, Pallas kernels for 0%

commit v1 on v0

v1 whole, which is shorter than its diff:
```python
import functools

import jax
import jax.numpy as jnp
from jax import lax
from jax.experimental import pallas as pl
from jax.experimental.pallas import tpu as pltpu
from jax.sharding import PartitionSpec as P

HEAD_DIM = 128
BLOCK = 128
MESH = pl.DeviceIdType.MESH
BF16 = jnp.bfloat16
F32 = jnp.float32
NT = (((1,), (1,)), ((), ()))


def place(seqs, heads):
    seq, head = lax.axis_index("seq"), lax.axis_index("head")
    return seq // 2, lax.rem(seq, 2) * heads + head, seqs // 2


def member(group, rank, heads):
    return (group * 2 + rank // heads, lax.rem(rank, heads))


def greet(seqs, heads):
    group, rank, groups = place(seqs, heads)
    size = 2 * heads
    barrier = pltpu.get_barrier_semaphore()
    targets = [member(group, lax.rem(rank + k, size), heads) for k in range(1, size)]
    targets += [member(lax.rem(group + d, groups), rank, heads) for d in (1, groups - 1)]
    for target in targets:
        pl.semaphore_signal(barrier, inc=1, device_id=target, device_id_type=MESH)
    pl.semaphore_wait(barrier, len(targets))


def gather_kernel(seqs, heads, *refs):
    sources, wins, (s1, r1, s2, r2, own_sem) = refs[:4], refs[4:8], refs[8:]
    group, rank, groups = place(seqs, heads)
    size = 2 * heads
    tok, cols = sources[0].shape[0], sources[0].shape[1] // size
    greet(seqs, heads)

    def here(a, piece):
        return pl.ds(pl.multiple_of((piece + (heads if a < 2 else 0)) * tok, tok), tok)

    def columns(r):
        return pl.ds(pl.multiple_of(r * cols, cols), cols)

    first, own = {}, []
    for a in range(4):
        copy = pltpu.make_async_copy(
            sources[a].at[:, columns(rank)], wins[a].at[here(a, rank), :], own_sem.at[a]
        )
        copy.start()
        own.append(copy)
        for k in range(1, size):
            peer = lax.rem(rank + k, size)
            copy = pltpu.make_async_remote_copy(
                src_ref=sources[a].at[:, columns(peer)],
                dst_ref=wins[a].at[here(a, rank), :],
                send_sem=s1.at[a, k],
                recv_sem=r1.at[a, k],
                device_id=member(group, peer, heads),
                device_id_type=MESH,
            )
            copy.start()
            first[a, k] = copy
    second = []
    for a in range(2):
        for k in range(size):
            if k == 0:
                own[a].wait()
            else:
                first[a, k].wait_recv()
            piece = lax.rem(rank - k + size, size)
            other = lax.rem(group + 2 * (piece // heads) - 1 + groups, groups)
            row = lax.rem(piece + 3 * heads, 4 * heads)
            copy = pltpu.make_async_remote_copy(
                src_ref=wins[a].at[here(a, piece), :],
                dst_ref=wins[a].at[pl.ds(pl.multiple_of(row * tok, tok), tok), :],
                send_sem=s2.at[a, k],
                recv_sem=r2.at[a, k],
                device_id=member(other, rank, heads),
                device_id_type=MESH,
            )
            copy.start()
            second.append(copy)
    for a in range(2, 4):
        own[a].wait()
        for k in range(1, size):
            first[a, k].wait_recv()
    for copy in first.values():
        copy.wait_send()
    for copy in second:
        copy.wait()


def attend_kernel(ids, used, q_ref, g_ref, k_ref, v_ref, o_ref, dq_ref, dk_ref, dv_ref, kt, vt, dk, dv):
    b = pl.program_id(1)
    slots = ids.shape[1]
    scale = HEAD_DIM**-0.5

    @pl.when(b == 0)
    def _():
        dk[...] = jnp.zeros_like(dk)
        dv[...] = jnp.zeros_like(dv)
        kt[...] = k_ref[...].T
        vt[...] = v_ref[...].T

    count = used[b]

    def visit(n):
        rows = [pl.ds(pl.multiple_of(ids[b, i] * BLOCK, BLOCK), BLOCK) for i in range(n)]
        q, g = q_ref[...], g_ref[...]
        keys = jnp.concatenate([k_ref[r, :] for r in rows], 0)
        values = jnp.concatenate([v_ref[r, :] for r in rows], 0)
        scores = lax.dot_general(keys, q, NT, preferred_element_type=F32) * scale
        slot = lax.broadcasted_iota(jnp.int32, scores.shape, 0) // BLOCK
        scores = jnp.where(slot < count, scores, -jnp.inf)
        raised = jnp.exp(scores - jnp.max(scores, axis=0, keepdims=True))
        weights = raised * (1.0 / jnp.sum(raised, axis=0, keepdims=True))
        low = weights.astype(BF16)
        vgt = jnp.concatenate([vt[:, r] for r in rows], 1)
        out = jnp.dot(vgt, low, preferred_element_type=F32).astype(BF16).astype(F32)
        o_ref[...] = out.T.astype(BF16)
        inner = jnp.sum(out * g.astype(F32).T, axis=0, keepdims=True)
        grad = lax.dot_general(values, g, NT, preferred_element_type=F32)
        grad_low = (weights * (grad - inner)).astype(BF16)
        kgt = jnp.concatenate([kt[:, r] for r in rows], 1)
        dqt = jnp.dot(kgt, grad_low, preferred_element_type=F32) * scale
        dq_ref[...] = dqt.T.astype(BF16)
        part_k = jnp.dot(grad_low, q, preferred_element_type=F32)
        part_v = jnp.dot(low, g, preferred_element_type=F32)
        for i, r in enumerate(rows):
            dk[r, :] += part_k[i * BLOCK : (i + 1) * BLOCK]
            dv[r, :] += part_v[i * BLOCK : (i + 1) * BLOCK]

    for n in range(2, slots + 1, 2):
        pl.when((count <= n) & (count > n - 2))(functools.partial(visit, n))

    @pl.when(b == pl.num_programs(1) - 1)
    def _():
        dk_ref[...] = (dk[...] * scale).astype(BF16)
        dv_ref[...] = dv[...].astype(BF16)


def return_kernel(seqs, heads, *refs):
    (att, gq, gk, gv), outs = refs[:4], refs[4:8]
    halo, mine, s1, r1, s2, r2, own_sem, load_sem = refs[8:]
    group, rank, groups = place(seqs, heads)
    size = 2 * heads
    tok, cols = outs[0].shape[0], outs[0].shape[1] // size
    greet(seqs, heads)

    def rows(r):
        return pl.ds(pl.multiple_of(r * tok, tok), tok)

    to = pl.ds(pl.multiple_of(rank * cols, cols), cols)
    halos, loads, sent, own = {}, [], [], []
    for a, grad in enumerate((gk, gv)):
        load = pltpu.make_async_copy(
            grad.at[pl.ds(heads * tok, size * tok), :], mine.at[a], load_sem.at[a]
        )
        load.start()
        loads.append(load)
        for k in range(size):
            piece = lax.rem(rank + k, size)
            other = lax.rem(group + 1 - 2 * (piece // heads) + groups, groups)
            copy = pltpu.make_async_remote_copy(
                src_ref=grad.at[rows(lax.rem(piece + 3 * heads, 4 * heads)), :],
                dst_ref=halo.at[a, rows(piece), :],
                send_sem=s1.at[a, k],
                recv_sem=r1.at[a, k],
                device_id=member(other, rank, heads),
                device_id_type=MESH,
            )
            copy.start()
            halos[a, k] = copy

    def hand_over(a, k, source):
        peer = lax.rem(rank + k, size)
        if k == 0:
            copy = pltpu.make_async_copy(source, outs[a].at[:, to], own_sem.at[a])
            own.append(copy)
        else:
            copy = pltpu.make_async_remote_copy(
                src_ref=source,
                dst_ref=outs[a].at[:, to],
                send_sem=s2.at[a, k],
                recv_sem=r2.at[a, k],
                device_id=member(group, peer, heads),
                device_id_type=MESH,
            )
            sent.append(copy)
        copy.start()

    for a, value in enumerate((att, gq)):
        for k in range(size):
            hand_over(a, k, value.at[rows(lax.rem(rank + k, size)), :])
    for a in range(2):
        loads[a].wait()
        for k in range(size):
            halos[a, k].wait_recv()
            piece = rows(lax.rem(rank + k, size))
            total = mine[a, piece, :].astype(F32) + halo[a, piece, :].astype(F32)
            mine[a, piece, :] = total.astype(BF16)
            hand_over(a + 2, k, mine.at[a, piece, :])
    for copy in halos.values():
        copy.wait_send()
    for copy in sent + own:
        copy.wait()


def local(seqs, heads, queries, key_rows, value_rows, cotangent, neighbours, counts):
    tok, width = queries.shape
    size = 2 * heads
    cols = width // size
    inner, window = size * tok, 2 * size * tok
    blocks = inner // BLOCK
    anywhere = pl.BlockSpec(memory_space=pl.ANY)
    dma = pltpu.SemaphoreType.DMA

    kw, vw, qw, gw = pl.pallas_call(
        functools.partial(gather_kernel, seqs, heads),
        out_shape=[jax.ShapeDtypeStruct((n, cols), BF16) for n in (window, window, inner, inner)],
        in_specs=[anywhere] * 4,
        out_specs=[anywhere] * 4,
        scratch_shapes=[dma((4, size)), dma((4, size)), dma((2, size)), dma((2, size)), dma((4,))],
        compiler_params=pltpu.CompilerParams(collective_id=0, has_side_effects=True),
        name="gather",
    )(key_rows, value_rows, queries, cotangent)

    first = lax.axis_index("seq") // 2 * blocks
    total = neighbours.shape[0]
    ids = lax.dynamic_slice_in_dim(neighbours, first, blocks, 0)
    ids = (ids - first + blocks // 2) % total
    used = lax.dynamic_slice_in_dim(counts, first, blocks, 0)
    tile = pl.BlockSpec((BLOCK, HEAD_DIM), lambda c, b, *_: (b, c))
    whole = pl.BlockSpec((window, HEAD_DIM), lambda c, b, *_: (0, c))
    att, gq, gk, gv = pl.pallas_call(
        attend_kernel,
        out_shape=[jax.ShapeDtypeStruct((n, cols), BF16) for n in (inner, inner, window, window)],
        grid_spec=pltpu.PrefetchScalarGridSpec(
            num_scalar_prefetch=2,
            grid=(cols // HEAD_DIM, blocks),
            in_specs=[tile, tile, whole, whole],
            out_specs=[tile, tile, whole, whole],
            scratch_shapes=[
                pltpu.VMEM((HEAD_DIM, window), BF16),
                pltpu.VMEM((HEAD_DIM, window), BF16),
                pltpu.VMEM((window, HEAD_DIM), F32),
                pltpu.VMEM((window, HEAD_DIM), F32),
            ],
        ),
        compiler_params=pltpu.CompilerParams(vmem_limit_bytes=50 * 2**20),
        name="attend",
    )(ids, used, qw, gw, kw, vw)

    return pl.pallas_call(
        functools.partial(return_kernel, seqs, heads),
        out_shape=[jax.ShapeDtypeStruct((tok, width), BF16)] * 4,
        in_specs=[anywhere] * 4,
        out_specs=[anywhere] * 4,
        scratch_shapes=[
            pltpu.VMEM((2, inner, cols), BF16),
            pltpu.VMEM((2, inner, cols), BF16),
            dma((2, size)),
            dma((2, size)),
            dma((4, size)),
            dma((4, size)),
            dma((4,)),
            dma((2,)),
        ],
        compiler_params=pltpu.CompilerParams(
            collective_id=1, has_side_effects=True, vmem_limit_bytes=50 * 2**20
        ),
        name="give_back",
    )(att, gq, gk, gv)


def solution(mesh):
    rows = P(("seq", "head"), None)
    return jax.shard_map(
        functools.partial(local, mesh.shape["seq"], mesh.shape["head"]),
        mesh=mesh,
        in_specs=(rows, rows, rows, rows, P(), P()),
        out_specs=(rows,) * 4,
        check_vma=False,
    )
```

time: 1200 us -> 304 us (0.25)
  waiting for transfers between devices: 534 us -> 0 us
  local copies, waits for them, and re-layouts: 312 us -> 10.6 us
  Pallas kernels: 0 us -> 290 us
  other arithmetic: 191 us -> 0.01 us
  matrix products: 70.2 us -> 0 us
  starting transfers between devices: 47.6 us -> 0 us
  blocking collectives: 29.3 us -> 0 us
    ppermute x4 -> x0, waiting for transfers between devices: 431 us -> none  [the longest x2 317 us: passed_along(): return lax.ppermute(value, axis, pairs)]
    pallas_call x0 -> x3, Pallas kernels: none -> 290 us  [the longest x1 111 us: local(): pl.pallas_call(functools.partial(return_kernel, seqs, heads), out_shape=[...]
    scatter-add x16 -> x0, other arithmetic: 151 us -> none  [the longest x8 75.8 us: visit(): grad_k = grad_k.at[tile_ids].add(outcome[2])]
    gather x32 -> x0, local copies, waits for them, and re-layouts: 107 us -> none  [the longest x16 72.7 us: visit(): value_window[tile_ids]]
    all_to_all x7 -> x0, waiting for transfers between devices: 104 us -> none  [the longest x1 21.6 us: local(): lax.all_to_all(grad_v_rows, 'head', split_axis=0, concat_axis=1, tiled=True)]
    dot_general x40 -> x0, matrix products: 64.5 us -> none  [the longest x8 25.8 us: tile_grads(): jnp.einsum('hqnk,qhd->nkhd', weights_low, g_tile, preferred_element_type=...]
    transpose x8 -> x0, local copies, waits for them, and re-layouts: 44.5 us -> none  [tile_grads(): jnp.einsum('hqnk,qhd->nkhd', weights_low, g_tile, preferred_element_type=...]
    all_to_all x7 -> x0, starting transfers between devices: 43.8 us -> none  [the longest x1 7.37 us: local(): lax.all_to_all(grad_v_rows, 'head', split_axis=0, concat_axis=1, tiled=True)]
  transfers between devices with their start and end apart: 11 -> 0, of which waited for: 9 -> 0; matrix products, arithmetic and copies ran while one was open for 5% -> 0% of each run, Pallas kernels for 0% -> 0%
where the time goes in v1:
time: 304 us; the launch traced here: 301 us
  Pallas kernels  290 us (95%)
  local copies, waits for them, and re-layouts  10.6 us (3%)
    pallas_call x1, Pallas kernels, local(): pl.pallas_call(functools.partial(return_kernel, seqs, heads), out_shape=[...  111 us
    pallas_call x1, Pallas kernels, local(): pl.pallas_call(functools.partial(gather_kernel, seqs, heads), out_shape=[...  103 us
    pallas_call x1, Pallas kernels, local(): pl.pallas_call(attend_kernel, out_shape=[jax.ShapeDtypeStruct((n, cols),...  76.4 us
    unnamed x15, local copies, waits for them, and re-layouts  9.75 us

profile of v1, /device:TPU:23, one launch (start us, length us, event | category | flops | bytes accessed | tf_op | source)
XLA Modules:
  0.0 301.4 jit_solution(1908130166597916165)
XLA Ops:
  0.6 0.0 copy-start
  0.7 0.7 dynamic_slice.7.used
  1.4 0.0 copy-done
  1.4 0.1 constant_dynamic-slice_fusion
  1.5 0.1 copy.11
  1.6 103.0 %gather.1 = (bf16[4096,512]{1,0:T(8,128)(2,1)}, bf16[4096,512]{1,0:T(8,128)(2,1)}, bf16[2048,512]{1,0:T(8,128)(2,1)}, bf16[2048,512]{1,0:T(8,128)(2,1)}) custom-call(bf16[256,4096]{1,0:T(8,128)(2,1)} %refs_0_.1, bf16[256,4096]{1,0:T(8,128)(2,1)} %refs_1_.1, bf16[256,4096]{1,0:T(8,128)(2,1)} %refs_2_.1, bf16[256,4096]{1,0:T(8,128)(2,1)} %refs_3_.1), custom_call_target="tpu_custom_call" | custom-call | tf_op jit(solution)/shard_map/gather/pallas_call | solution.py:225
  104.5 76.4 %attend.1 = (bf16[2048,512]{1,0:T(8,128)(2,1)S(1)}, bf16[2048,512]{1,0:T(8,128)(2,1)}, bf16[4096,512]{1,0:T(8,128)(2,1)}, bf16[4096,512]{1,0:T(8,128)(2,1)}) custom-call(s32[16,8]{1,0:T(8,128)S(1)} %add_select_fusion.ids, s32[16]{0:T(128)S(1)} %dynamic_slice.7.used, bf16[2048,512]{1,0:T(8,128)(2,1)} %get-tuple-element.12.q_ref, ...), custom_call_target="tpu_custom_call" | custom-call | tf_op jit(solution)/shard_map/attend/pallas_call | solution.py:242
  180.9 0.0 copy-start.1
  180.9 1.3 copy-done.1
  182.2 110.8 %give_back.1 = (bf16[256,4096]{1,0:T(8,128)(2,1)S(1)}, bf16[256,4096]{1,0:T(8,128)(2,1)}, bf16[256,4096]{1,0:T(8,128)(2,1)}, bf16[256,4096]{1,0:T(8,128)(2,1)}) custom-call(bf16[2048,512]{1,0:T(8,128)(2,1)} %copy-done.1, bf16[2048,512]{1,0:T(8,128)(2,1)} %get-tuple-element.17.refs_1_, bf16[4096,512]{1,0:T(8,128)(2,1)} %get-tuple-element.18.refs_2_, ...), custom_call_target="tpu_custom_call" | custom-call | tf_op jit(solution)/shard_map/give_back/pallas_call | solution.py:261
  293.0 0.0 copy-start.4
  293.1 1.3 copy.16
  294.4 1.0 copy-done.4
  295.4 0.0 copy-start.3
  295.4 1.3 copy.17
  296.7 1.0 copy-done.3
  297.7 0.0 copy-start.2
  297.7 1.3 copy.18
  299.1 1.0 copy-done.2
  300.1 1.3 copy.19
  (1 shorter events, 0.0 us)
Async XLA Ops:
  0.6 0.8 copy-start
  180.9 1.3 copy-start.1
  293.0 2.3 copy-start.4
  295.4 2.3 copy-start.3
  297.7 2.3 copy-start.2

commit v2 on v0

v2 whole, which is shorter than its diff:
```python
import functools

import jax
import jax.numpy as jnp
from jax import lax
from jax.experimental import pallas as pl
from jax.experimental.pallas import tpu as pltpu
from jax.sharding import PartitionSpec as P

HEAD_DIM = 128
BLOCK = 128
MESH = pl.DeviceIdType.MESH
BF16 = jnp.bfloat16
F32 = jnp.float32
NT = (((1,), (1,)), ((), ()))


def place(seqs, heads):
    seq, head = lax.axis_index("seq"), lax.axis_index("head")
    return seq // 2, lax.rem(seq, 2) * heads + head, seqs // 2


def member(group, rank, heads):
    return (group * 2 + rank // heads, lax.rem(rank, heads))


def greet(seqs, heads):
    group, rank, groups = place(seqs, heads)
    size = 2 * heads
    barrier = pltpu.get_barrier_semaphore()
    targets = [member(group, lax.rem(rank + k, size), heads) for k in range(1, size)]
    targets += [member(lax.rem(group + d, groups), rank, heads) for d in (1, groups - 1)]
    for target in targets:
        pl.semaphore_signal(barrier, inc=1, device_id=target, device_id_type=MESH)
    pl.semaphore_wait(barrier, len(targets))


def layer_kernel(seqs, heads, ids, used, named, *refs):
    sources, outs = refs[:4], refs[4:8]
    kv, qs, gs, kvw, kvt, part, att, gq, grads, halo = refs[8:18]
    s1, r1, own1, s2, r2, s3, r3, s4, r4, own4 = refs[18:]
    group, rank, groups = place(seqs, heads)
    size = 2 * heads
    tok = sources[0].shape[0]
    planes, window = kv.shape[0], kv.shape[1] // BLOCK
    blocks = window // 2
    slots = ids.shape[0] // blocks
    cols = planes * HEAD_DIM
    per = -(-2 * size // blocks)
    scale = HEAD_DIM**-0.5
    low_lanes, high_lanes = pl.ds(0, HEAD_DIM), pl.ds(HEAD_DIM, HEAD_DIM)

    def rows(r):
        return pl.ds(pl.multiple_of(r * tok, tok), tok)

    def columns(r, c):
        return pl.ds(pl.multiple_of(r * cols + c * HEAD_DIM, HEAD_DIM), HEAD_DIM)

    def copy_to(source, target, sends, receives, device):
        return pltpu.make_async_remote_copy(
            src_ref=source,
            dst_ref=target,
            send_sem=sends,
            recv_sem=receives,
            device_id=device,
            device_id_type=MESH,
        )

    def first(c, a, k):
        peer = lax.rem(rank + k, size)
        source = sources[a].at[:, columns(peer, c)]
        if a < 2:
            target = kv.at[c, rows(rank + heads), (low_lanes, high_lanes)[a]]
        else:
            target = (qs, gs)[a - 2].at[c, rows(rank), :]
        if k == 0:
            return pltpu.make_async_copy(source, target, own1.at[c, a])
        return copy_to(source, target, s1.at[c, a, k], r1.at[c, a, k], member(group, peer, heads))

    def arrive(copy, k):
        if k == 0:
            copy.wait()
        else:
            copy.wait_recv()

    def second(c, k):
        piece = lax.rem(rank - k + size, size)
        other = lax.rem(group + 2 * (piece // heads) - 1 + groups, groups)
        return copy_to(
            kv.at[c, rows(piece + heads), :],
            kv.at[c, rows(lax.rem(piece + 3 * heads, 4 * heads)), :],
            s2.at[c, k],
            r2.at[c, k],
            member(other, rank, heads),
        )

    def forward(c, k):
        arrive(first(c, 0, k), k)
        arrive(first(c, 1, k), k)
        second(c, k).start()

    def third(c, k):
        piece = lax.rem(rank + k, size)
        other = lax.rem(group + 1 - 2 * (piece // heads) + groups, groups)
        return copy_to(
            grads.at[c, rows(lax.rem(piece + 3 * heads, 4 * heads)), :],
            halo.at[c, rows(piece), :],
            s3.at[c, k],
            r3.at[c, k],
            member(other, rank, heads),
        )

    def fourth(c, a, k):
        peer = lax.rem(rank + k, size)
        if a < 2:
            source = (att, gq)[a].at[c, rows(peer), :]
        else:
            source = grads.at[c, rows(peer + heads), (low_lanes, high_lanes)[a - 2]]
        target = outs[a].at[:, columns(rank, c)]
        if k == 0:
            return pltpu.make_async_copy(source, target, own4.at[c, a])
        return copy_to(source, target, s4.at[c, a, k], r4.at[c, a, k], member(group, peer, heads))

    def settle(c, k):
        third(c, k).wait_recv()
        piece = lax.rem(rank + k, size)
        mine = rows(piece + heads)
        total = grads[c, mine, :].astype(F32) + halo[c, rows(piece), :].astype(F32)
        grads[c, mine, :] = total.astype(BF16)
        fourth(c, 2, k).start()
        fourth(c, 3, k).start()

    greet(seqs, heads)

    def begin(c, _):
        for a in range(4):
            for k in range(size):
                first(c, a, k).start()
        return 0

    lax.fori_loop(0, planes, begin, 0)
    part[blocks * slots] = jnp.zeros(part.shape[1:], F32)
    for k in range(size):
        forward(0, k)

    def attend(c, b):
        picks = [ids[b * slots + i] for i in range(slots)]
        here = pl.ds(pl.multiple_of(b * BLOCK, BLOCK), BLOCK)
        q, g = qs[c, here, :], gs[c, here, :]
        none = jnp.zeros_like(q)
        both = jnp.concatenate(
            [jnp.concatenate([q, none], 1), jnp.concatenate([none, g], 1)], 0
        )
        tiles = jnp.concatenate([kvw[p] for p in picks], 0)
        product = lax.dot_general(tiles, both, NT, preferred_element_type=F32)
        slot = lax.broadcasted_iota(jnp.int32, (slots * BLOCK, HEAD_DIM), 0) // BLOCK
        scores = jnp.where(slot < used[b], product[:, :HEAD_DIM] * scale, -jnp.inf)
        raised = jnp.exp(scores - jnp.max(scores, axis=0, keepdims=True))
        weights = raised * (1.0 / jnp.sum(raised, axis=0, keepdims=True))
        low = weights.astype(BF16)
        vgt = jnp.concatenate([kvt[p, high_lanes, :] for p in picks], 1)
        out = jnp.dot(vgt, low, preferred_element_type=F32).astype(BF16).astype(F32)
        att[c, here, :] = out.T.astype(BF16)
        inner = jnp.sum(out * g.astype(F32).T, axis=0, keepdims=True)
        grad_low = (weights * (product[:, HEAD_DIM:] - inner)).astype(BF16)
        kgt = jnp.concatenate([kvt[p, low_lanes, :] for p in picks], 1)
        dqt = jnp.dot(kgt, grad_low, preferred_element_type=F32) * scale
        gq[c, here, :] = dqt.T.astype(BF16)
        pair = jnp.concatenate([grad_low, low], 1)
        sums = jnp.dot(pair, both, preferred_element_type=F32)
        part[pl.ds(b * slots, slots)] = sums.reshape((slots, BLOCK, 2 * HEAD_DIM))

    def plane(c, _):
        for k in range(size):
            second(c, k).wait_recv()
            for a in (2, 3):
                arrive(first(c, a, k), k)

        def prepare(w, _):
            tile = kv[c, pl.ds(pl.multiple_of(w * BLOCK, BLOCK), BLOCK), :]
            kvw[w] = tile
            kvt[w] = tile.T
            return 0

        lax.fori_loop(0, window, prepare, 0)

        def step(b, _):
            for k in range(size):
                pl.when((b == k // per) & (c + 1 < planes))(functools.partial(forward, c + 1, k))
                pl.when((b == blocks // 2 + k // per) & (c > 0))(
                    functools.partial(settle, c - 1, k)
                )
            attend(c, b)
            return 0

        lax.fori_loop(0, blocks, step, 0)

        def collect(w, _):
            def add(b, total):
                return total + part[named[w * blocks + b]]

            total = lax.fori_loop(
                jnp.maximum(0, w - blocks),
                jnp.minimum(blocks - 1, w) + 1,
                add,
                jnp.zeros((BLOCK, 2 * HEAD_DIM), F32),
            )
            lane = lax.broadcasted_iota(jnp.int32, total.shape, 1)
            total = total * jnp.where(lane < HEAD_DIM, scale, 1.0)
            grads[c, pl.ds(pl.multiple_of(w * BLOCK, BLOCK), BLOCK), :] = total.astype(BF16)
            return 0

        lax.fori_loop(0, window, collect, 0)
        for k in range(size):
            third(c, k).start()
        for k in range(size):
            for a in range(2):
                fourth(c, a, k).start()
        return 0

    lax.fori_loop(0, planes, plane, 0)
    for k in range(size):
        settle(planes - 1, k)

    def finish(c, _):
        for k in range(size):
            second(c, k).wait_send()
            third(c, k).wait_send()
            for a in range(4):
                if k:
                    first(c, a, k).wait_send()
                fourth(c, a, k).wait()
        return 0

    lax.fori_loop(0, planes, finish, 0)


def local(seqs, heads, queries, key_rows, value_rows, cotangent, neighbours, counts):
    tok, width = queries.shape
    size = 2 * heads
    planes = width // size // HEAD_DIM
    inner, window = size * tok, 2 * size * tok
    blocks = inner // BLOCK
    slots = neighbours.shape[1]
    anywhere = pl.BlockSpec(memory_space=pl.ANY)
    scalars = pl.BlockSpec(memory_space=pltpu.SMEM)
    dma = pltpu.SemaphoreType.DMA

    start = lax.axis_index("seq") // 2 * blocks
    ids = lax.dynamic_slice_in_dim(neighbours, start, blocks, 0)
    ids = (ids - start + blocks // 2) % neighbours.shape[0]
    used = lax.dynamic_slice_in_dim(counts, start, blocks, 0)
    slot = jnp.arange(slots, dtype=jnp.int32)
    entry = jnp.arange(blocks, dtype=jnp.int32)[:, None] * slots + slot[None, :]
    match = ids[None] == jnp.arange(2 * blocks, dtype=jnp.int32)[:, None, None]
    match = match & (slot[None, :] < used[:, None])[None]
    named = jnp.min(jnp.where(match, entry[None], blocks * slots), axis=2)

    return pl.pallas_call(
        functools.partial(layer_kernel, seqs, heads),
        out_shape=[jax.ShapeDtypeStruct((tok, width), BF16)] * 4,
        in_specs=[scalars] * 3 + [anywhere] * 4,
        out_specs=[anywhere] * 4,
        scratch_shapes=[
            pltpu.VMEM((planes, window, 2 * HEAD_DIM), BF16),
            pltpu.VMEM((planes, inner, HEAD_DIM), BF16),
            pltpu.VMEM((planes, inner, HEAD_DIM), BF16),
            pltpu.VMEM((2 * blocks, BLOCK, 2 * HEAD_DIM), BF16),
            pltpu.VMEM((2 * blocks, 2 * HEAD_DIM, BLOCK), BF16),
            pltpu.VMEM((blocks * slots + 1, BLOCK, 2 * HEAD_DIM), F32),
            pltpu.VMEM((planes, inner, HEAD_DIM), BF16),
            pltpu.VMEM((planes, inner, HEAD_DIM), BF16),
            pltpu.VMEM((planes, window, 2 * HEAD_DIM), BF16),
            pltpu.VMEM((planes, inner, 2 * HEAD_DIM), BF16),
            dma((planes, 4, size)),
            dma((planes, 4, size)),
            dma((planes, 4)),
            dma((planes, size)),
            dma((planes, size)),
            dma((planes, size)),
            dma((planes, size)),
            dma((planes, 4, size)),
            dma((planes, 4, size)),
            dma((planes, 4)),
        ],
        compiler_params=pltpu.CompilerParams(
            collective_id=0, has_side_effects=True, vmem_limit_bytes=60 * 2**20
        ),
        name="layer",
    )(
        ids.reshape(-1),
        used,
        named.reshape(-1),
        key_rows,
        value_rows,
        queries,
        cotangent,
    )


def solution(mesh):
    rows = P(("seq", "head"), None)
    return jax.shard_map(
        functools.partial(local, mesh.shape["seq"], mesh.shape["head"]),
        mesh=mesh,
        in_specs=(rows, rows, rows, rows, P(), P()),
        out_specs=(rows,) * 4,
        check_vma=False,
    )
```

time: 1200 us -> 240 us (0.20)
  waiting for transfers between devices: 534 us -> 0 us
  local copies, waits for them, and re-layouts: 312 us -> 11.4 us
  Pallas kernels: 0 us -> 223 us
  other arithmetic: 191 us -> 1.05 us
  matrix products: 70.2 us -> 0 us
  starting transfers between devices: 47.6 us -> 0 us
  blocking collectives: 29.3 us -> 0 us
    ppermute x4 -> x0, waiting for transfers between devices: 431 us -> none  [the longest x2 317 us: passed_along(): return lax.ppermute(value, axis, pairs)]
    pallas_call x0 -> x1, Pallas kernels: none -> 223 us  [local(): pl.pallas_call(functools.partial(layer_kernel, seqs, heads), out_shape=[j...]
    scatter-add x16 -> x0, other arithmetic: 151 us -> none  [the longest x8 75.8 us: visit(): grad_k = grad_k.at[tile_ids].add(outcome[2])]
    gather x32 -> x0, local copies, waits for them, and re-layouts: 107 us -> none  [the longest x16 72.7 us: visit(): value_window[tile_ids]]
    all_to_all x7 -> x0, waiting for transfers between devices: 104 us -> none  [the longest x1 21.6 us: local(): lax.all_to_all(grad_v_rows, 'head', split_axis=0, concat_axis=1, tiled=True)]
    dot_general x40 -> x0, matrix products: 64.5 us -> none  [the longest x8 25.8 us: tile_grads(): jnp.einsum('hqnk,qhd->nkhd', weights_low, g_tile, preferred_element_type=...]
    transpose x8 -> x0, local copies, waits for them, and re-layouts: 44.5 us -> none  [tile_grads(): jnp.einsum('hqnk,qhd->nkhd', weights_low, g_tile, preferred_element_type=...]
    all_to_all x7 -> x0, starting transfers between devices: 43.8 us -> none  [the longest x1 7.37 us: local(): lax.all_to_all(grad_v_rows, 'head', split_axis=0, concat_axis=1, tiled=True)]
  transfers between devices with their start and end apart: 11 -> 0, of which waited for: 9 -> 0; matrix products, arithmetic and copies ran while one was open for 5% -> 0% of each run, Pallas kernels for 0% -> 0%
where the time goes in v2:
time: 240 us; the launch traced here: 236 us
  Pallas kernels  223 us (93%)
  local copies, waits for them, and re-layouts  11.4 us (5%)
    pallas_call x1, Pallas kernels, local(): pl.pallas_call(functools.partial(layer_kernel, seqs, heads), out_shape=[j...  223 us
    unnamed x12, local copies, waits for them, and re-layouts  9.3 us

profile of v2, /device:TPU:23, one launch (start us, length us, event | category | flops | bytes accessed | tf_op | source)
XLA Modules:
  0.0 235.9 jit_solution(16818307018071618632)
XLA Ops:
  0.6 0.7 dynamic_slice.7.used
  1.4 0.0 copy-start.3
  1.4 0.1 iota_compare_fusion.1
  1.5 0.8 add_select_fusion
  2.2 0.1 copy.14
  2.3 0.6 reshape.57.ids
  2.9 0.1 iota_add_fusion
  3.0 0.1 select_reduce_fusion
  3.1 0.1 copy.16
  3.2 0.7 reshape.58.named
  3.9 0.0 copy-done.3
  3.9 222.7 %layer.1 = (bf16[256,4096]{1,0:T(8,128)(2,1)}, bf16[256,4096]{1,0:T(8,128)(2,1)}, bf16[256,4096]{1,0:T(8,128)(2,1)}, bf16[256,4096]{1,0:T(8,128)(2,1)}) custom-call(s32[128]{0:T(128)} %reshape.57.ids, s32[16]{0:T(128)} %copy-done.3, s32[512]{0:T(512)} %reshape.58.named, bf16[256,4096]{1,0:T(8,128)(2,1)} %refs_0_.1, bf16[256,4096]{1,0:T(8,128)(2,1)} %refs_1_.1, ...), custom_call_target="tpu_custom_call" | custom-call | tf_op jit(solution)/shard_map/layer/pallas_call | solution.py:259
  226.6 0.0 copy-start.2
  226.6 3.3 %copy.21 = bf16[256,4096]{1,0:T(8,128)(2,1)} copy(bf16[256,4096]{1,0:T(8,128)(2,1)} %get-tuple-element.8) | data formatting | bytes 4194304
  229.9 0.0 copy-done.2
  229.9 0.0 copy-start.1
  229.9 1.3 copy.22
  231.2 1.0 copy-done.1
  232.2 0.0 copy-start
  232.2 1.3 copy.23
  233.5 1.0 copy-done
  234.6 1.3 copy.24
  (1 shorter events, 0.0 us)
Async XLA Ops:
  1.4 2.5 %copy-start.3 = (s32[16]{0:T(128)}, s32[16]{0:T(128)S(1)}, u32[]{:S(2)}) copy-start(s32[16]{0:T(128)S(1)} %dynamic_slice.7.used) | copy-start | bytes 196
  226.6 3.3 %copy-start.2 = (bf16[256,4096]{1,0:T(8,128)(2,1)S(1)}, bf16[256,4096]{1,0:T(8,128)(2,1)}, u32[]{:S(2)}) copy-start(bf16[256,4096]{1,0:T(8,128)(2,1)} %get-tuple-element.9) | copy-start | bytes 6291460
  229.9 2.3 copy-start.1
  232.2 2.3 copy-start

commit v3 on v2

--- a/solution.py
+++ b/solution.py
@@ -139,8 +139,19 @@
         return 0
 
     lax.fori_loop(0, planes, begin, 0)
-    part[blocks * slots] = jnp.zeros(part.shape[1:], F32)
-    for k in range(size):
+
+    def clear(i, _):
+        part[i] = jnp.zeros(part.shape[1:], F32)
+        return 0
+
+    lax.fori_loop(0, part.shape[0], clear, 0)
+
+    def lead(c, _):
+        forward(c, 0)
+        return 0
+
+    lax.fori_loop(0, planes, lead, 0)
+    for k in range(1, size):
         forward(0, k)
 
     def attend(c, b):
@@ -186,14 +197,19 @@
 
         def step(b, _):
             for k in range(size):
-                pl.when((b == k // per) & (c + 1 < planes))(functools.partial(forward, c + 1, k))
+                if k:
+                    pl.when((b == k // per) & (c + 1 < planes))(
+                        functools.partial(forward, c + 1, k)
+                    )
                 pl.when((b == blocks // 2 + k // per) & (c > 0))(
                     functools.partial(settle, c - 1, k)
                 )
             attend(c, b)
+            for k in range(size):
+                for a in range(2):
+                    ready = (b + 1) * BLOCK == (lax.rem(rank + k, size) + 1) * tok
+                    pl.when(ready)(fourth(c, a, k).start)
             return 0
-
-        lax.fori_loop(0, blocks, step, 0)
 
         def collect(w, _):
             def add(b, total):
@@ -210,12 +226,16 @@
             grads[c, pl.ds(pl.multiple_of(w * BLOCK, BLOCK), BLOCK), :] = total.astype(BF16)
             return 0
 
-        lax.fori_loop(0, window, collect, 0)
+        half = blocks // 2
+        lax.fori_loop(0, half, step, 0)
+        lax.fori_loop(0, half, collect, 0)
         for k in range(size):
-            third(c, k).start()
+            pl.when(lax.rem(rank + k, size) >= heads)(third(c, k).start)
+        lax.fori_loop(half, blocks, step, 0)
+        lax.fori_loop(blocks + half, window, collect, 0)
         for k in range(size):
-            for a in range(2):
-                fourth(c, a, k).start()
+            pl.when(lax.rem(rank + k, size) < heads)(third(c, k).start)
+        lax.fori_loop(half, blocks + half, collect, 0)
         return 0
 
     lax.fori_loop(0, planes, plane, 0)

time: 240 us -> 225 us (0.938); the launches traced: 236 us -> 225 us
  Pallas kernels: 223 us -> 212 us
    pallas_call x1, Pallas kernels: 223 us -> 212 us  [local(): pl.pallas_call(functools.partial(layer_kernel, seqs, heads), out_shape=[j...]
where the time goes in v3:
time: 225 us
  Pallas kernels  212 us (94%)
  local copies, waits for them, and re-layouts  11.4 us (5%)
    pallas_call x1, Pallas kernels, local(): pl.pallas_call(functools.partial(layer_kernel, seqs, heads), out_shape=[j...  212 us
    unnamed x12, local copies, waits for them, and re-layouts  9.3 us

profile of v3, /device:TPU:23, one launch (start us, length us, event | category | flops | bytes accessed | tf_op | source)
XLA Modules:
  0.0 225.0 jit_solution(13483346161055054089)
XLA Ops:
  0.6 0.7 dynamic_slice.7.used
  1.4 0.0 copy-start.3
  1.4 0.1 iota_compare_fusion.1
  1.5 0.8 add_select_fusion
  2.2 0.1 copy.14
  2.3 0.6 reshape.57.ids
  2.9 0.1 iota_add_fusion
  3.0 0.1 select_reduce_fusion
  3.1 0.1 copy.16
  3.2 0.7 reshape.58.named
  3.9 0.0 copy-done.3
  3.9 211.8 %layer.1 = (bf16[256,4096]{1,0:T(8,128)(2,1)}, bf16[256,4096]{1,0:T(8,128)(2,1)}, bf16[256,4096]{1,0:T(8,128)(2,1)}, bf16[256,4096]{1,0:T(8,128)(2,1)}) custom-call(s32[128]{0:T(128)} %reshape.57.ids, s32[16]{0:T(128)} %copy-done.3, s32[512]{0:T(512)} %reshape.58.named, bf16[256,4096]{1,0:T(8,128)(2,1)} %refs_0_.1, bf16[256,4096]{1,0:T(8,128)(2,1)} %refs_1_.1, ...), custom_call_target="tpu_custom_call" | custom-call | tf_op jit(solution)/shard_map/layer/pallas_call | solution.py:279
  215.7 0.0 copy-start.2
  215.7 3.3 %copy.21 = bf16[256,4096]{1,0:T(8,128)(2,1)} copy(bf16[256,4096]{1,0:T(8,128)(2,1)} %get-tuple-element.8) | data formatting | bytes 4194304
  219.0 0.0 copy-done.2
  219.0 0.0 copy-start.1
  219.0 1.3 copy.22
  220.3 1.0 copy-done.1
  221.3 0.0 copy-start
  221.3 1.3 copy.23
  222.6 1.0 copy-done
  223.7 1.3 copy.24
  (1 shorter events, 0.0 us)
Async XLA Ops:
  1.4 2.5 %copy-start.3 = (s32[16]{0:T(128)}, s32[16]{0:T(128)S(1)}, u32[]{:S(2)}) copy-start(s32[16]{0:T(128)S(1)} %dynamic_slice.7.used) | copy-start | bytes 196
  215.7 3.3 %copy-start.2 = (bf16[256,4096]{1,0:T(8,128)(2,1)S(1)}, bf16[256,4096]{1,0:T(8,128)(2,1)}, u32[]{:S(2)}) copy-start(bf16[256,4096]{1,0:T(8,128)(2,1)} %get-tuple-element.9) | copy-start | bytes 6291460
  219.0 2.3 %copy-start.1 = (bf16[256,4096]{1,0:T(8,128)(2,1)S(1)}, bf16[256,4096]{1,0:T(8,128)(2,1)}, u32[]{:S(2)}) copy-start(bf16[256,4096]{1,0:T(8,128)(2,1)} %get-tuple-element.10) | copy-start | bytes 6291460
  221.3 2.3 %copy-start = (bf16[256,4096]{1,0:T(8,128)(2,1)S(1)}, bf16[256,4096]{1,0:T(8,128)(2,1)}, u32[]{:S(2)}) copy-start(bf16[256,4096]{1,0:T(8,128)(2,1)} %get-tuple-element.11) | copy-start | bytes 6291460
